TPU v7x, 32 devices: a whole 2x2x4 slice. The times are simulated.
32 devices in a mesh: snap: 8 (over y, x, core), clus: 4 (over z).
Axes of the slice: x: 2, y: 2, z: 4, core: 2. Of those that a mesh axis runs over, the one named last changes fastest.
Arguments:
- features: bfloat16 [32, 2048, 512], P('snap', 'clus'), parts along dimension 1, may hold values from -6 to 6
- adjacency: int32 [32, 2048, 512], P('snap', 'clus'), parts along dimension 1, may hold values 0 or 1
- first_seen: int32 [2048], P(('clus', 'snap')), parts along dimension 0, may hold values from 0 to 15
- pos_embed: bfloat16 [32, 512], replicated, may hold values from -3 to 3
- w_struct: bfloat16 [2, 512, 512], replicated, may hold values from -0.25 to 0.25
- w_query: bfloat16 [2, 512, 512], replicated, as said below
- w_key: bfloat16 [2, 512, 512], replicated, as said below
- w_value: bfloat16 [2, 512, 512], replicated, may hold values from -0.25 to 0.25
- w_out: bfloat16 [2, 512, 512], replicated, may hold values from -0.25 to 0.25
- w_up: bfloat16 [2, 512, 1024], replicated, may hold values from -0.25 to 0.25
- w_down: bfloat16 [2, 1024, 512], replicated, may hold values from -0.1875 to 0.1875
- norm_gain: float32 [2, 2, 512], replicated, may hold values from 0.1 to 1.9
Outputs:
- hidden_out: bfloat16 [32, 2048, 512], P('snap', 'clus'), parts along dimension 1
There are 4 independent parts, one for each index of `clus`. A program takes and returns all parts, laid end to end along the dimension named above; an argument that names none is the same for every part. Nothing has to cross between parts.
Inputs may be any that keep to these rules, and one draw needn't show every extreme that they name: `w_query`: entries lie within -30 / sqrt(512) to 30 / sqrt(512). `w_key`: entries lie within -5 / sqrt(512) to 5 / sqrt(512).
All inputs are finite; a program needn't handle non-finite values. No bound on the sum of `adjacency` on one device may be relied on, other than what follows from the above.
Results may differ from a plain program's by a relative error of at most 0.012.
Values may be sent and summed in bfloat16 or wider, within the bound.
A program may use at most 128 MiB of HBM per device.

v0:
```python
import jax
import jax.numpy as jnp
from jax import lax
from jax.sharding import PartitionSpec as P

HEADS = 8
BLOCKS = 2


def layer_norm(values_in, gain):
    average = jnp.mean(values_in, axis=-1, keepdims=True)
    centred = values_in - average
    scattered_rows = jnp.mean(centred * centred, axis=-1, keepdims=True)
    return centred * lax.rsqrt(scattered_rows + 1e-05) * gain


def convolve(hidden, adjacent, degree, weight_matrix):
    summed = jnp.einsum(
        "snm,smd->snd", adjacent, hidden, preferred_element_type=jnp.float32
    ) + hidden.astype(jnp.float32)
    blended_values = (summed / degree[..., None]).astype(jnp.bfloat16)
    convolved = jax.nn.elu(
        jnp.einsum("zfk,kb->zfb", blended_values, weight_matrix, preferred_element_type=jnp.float32)
    )
    return (convolved + hidden.astype(jnp.float32)).astype(jnp.bfloat16)


def temporal(
    vertex_rows, first_seen, pos_embed, w_query, w_key, w_value, w_out, w_up, w_down, gain_pair
):
    timestep_count, vertex_count, model_width = vertex_rows.shape
    head_count = w_struct_heads()
    head_dim = model_width // head_count
    row_totals = vertex_rows.astype(jnp.float32) + pos_embed.astype(jnp.float32)[:, None, :]
    row_totals = row_totals.reshape(-1, model_width)
    normed = layer_norm(row_totals, gain_pair[0]).astype(jnp.bfloat16)
    shape_heads = (timestep_count, vertex_count, head_count, head_dim)
    queries = (
        jnp.dot(normed, w_query, preferred_element_type=jnp.float32)
        .astype(jnp.bfloat16)
        .reshape(shape_heads)
    )
    key_rows = (
        jnp.dot(normed, w_key, preferred_element_type=jnp.float32)
        .astype(jnp.bfloat16)
        .reshape(shape_heads)
    )
    values = (
        jnp.dot(normed, w_value, preferred_element_type=jnp.float32)
        .astype(jnp.bfloat16)
        .reshape(shape_heads)
    )
    scores = jnp.einsum(
        "tvhd,jvhd->vhtj", queries, key_rows, preferred_element_type=jnp.float32
    ) * head_dim ** (-0.5)
    positions = jnp.arange(timestep_count, dtype=jnp.int32)
    causal = positions[None, :] <= positions[:, None]
    diagonal_mask = positions[None, :] == positions[:, None]
    present = positions[None, None, :] >= first_seen[:, None, None]
    allowed = causal[None] & (present | diagonal_mask[None])
    scores = jnp.where(allowed[:, None], scores, -1e30)
    weights = jax.nn.softmax(scores, axis=-1).astype(jnp.bfloat16)
    attended_heads = jnp.einsum(
        "vhtj,jvhd->tvhd", weights, values, preferred_element_type=jnp.float32
    )
    attended_heads = attended_heads.astype(jnp.bfloat16).reshape(-1, model_width)
    attended = row_totals + jnp.dot(attended_heads, w_out, preferred_element_type=jnp.float32)
    normed_two = layer_norm(attended, gain_pair[1]).astype(jnp.bfloat16)
    inner_rows = jax.nn.gelu(jnp.dot(normed_two, w_up, preferred_element_type=jnp.float32)).astype(
        jnp.bfloat16
    )
    finished = attended + jnp.dot(inner_rows, w_down, preferred_element_type=jnp.float32)
    return finished.astype(jnp.bfloat16).reshape(timestep_count, vertex_count, model_width)


def w_struct_heads():
    return HEADS


def on_device(
    features,
    adjacency,
    first_seen,
    pos_embed,
    w_struct,
    w_query,
    w_key,
    w_value,
    w_out,
    w_up,
    w_down,
    norm_gain,
):
    adjacent = adjacency.astype(jnp.bfloat16)
    degree = 1.0 + jnp.sum(adjacency, axis=2).astype(jnp.float32)
    hidden = features
    for layer in range(BLOCKS):
        weight_matrix = w_struct[layer]
        convolved = convolve(hidden, adjacent, degree, weight_matrix)
        vertex_rows = lax.all_to_all(convolved, "snap", split_axis=1, concat_axis=0, tiled=True)
        finished = temporal(
            vertex_rows,
            first_seen,
            pos_embed,
            w_query[layer],
            w_key[layer],
            w_value[layer],
            w_out[layer],
            w_up[layer],
            w_down[layer],
            norm_gain[layer],
        )
        hidden = lax.all_to_all(finished, "snap", split_axis=0, concat_axis=1, tiled=True)
    return hidden


def solution(mesh):
    in_specs = (
        P("snap", "clus", None),
        P("snap", "clus", None),
        P(("clus", "snap")),
        P(),
        P(),
        P(),
        P(),
        P(),
        P(),
        P(),
        P(),
        P(),
    )
    out_specs = P("snap", "clus", None)
    return jax.shard_map(
        on_device, mesh=mesh, in_specs=in_specs, out_specs=out_specs, check_vma=False
    )
```

profile of v0, /device:TPU:0, one launch (start us, length us, event | category | flops | bytes accessed | tf_op | source)
XLA Modules:
  0.0 295.9 jit_solution(11578212021589435395)
XLA Ops:
  0.0 2.6 reduce_sum.99
  2.7 7.9 %fusion.22 = bf16[4,512,512]{2,1,0:T(8,128)(2,1)S(1)} fusion(bf16[4,512,512]{2,1,0:T(8,128)(2,1)} %param.12, f32[4,512]{1,0:T(4,128)S(1)} %convert_add_fusion.4, s32[4,512,512]{2,1,0:T(8,128)} %param.13, bf16[2,512,512]{2,1,0:T(8,128)(2,1)S(1)} %copy-done.12), kind=kOutput, calls=%fused_computation.40 | convolution fusion | flops 2159017984 | bytes 13115392 | tf_op jit(solution)/shard_map/zfk,kb->zfb/dot_general | solution.py:23
  10.5 0.0 copy-start.7
  10.6 0.0 copy-start.11
  10.6 0.0 copy-start.8
  10.6 2.9 copy.80
  13.5 5.4 %all-to-all-start = ((bf16[4,512,512]{2,0,1:T(4,128)(2,1)}), bf16[4,512,512]{2,0,1:T(4,128)(2,1)S(1)}, u32[]{:S(2)}, u32[]{:S(2)}) async-start(bf16[4,512,512]{2,0,1:T(4,128)(2,1)} %copy.80), calls=%async_computation | async-start | bytes 4194304 | tf_op jit(solution)/shard_map/all_to_all | solution.py:100
  19.0 0.1 iota_compare_fusion
  19.1 0.6 fusion.134
  19.7 0.3 or_and_fusion
  20.1 25.5 %all-to-all-done = bf16[4,512,512]{2,0,1:T(4,128)(2,1)S(1)} async-done(((bf16[4,512,512]{2,0,1:T(4,128)(2,1)}), bf16[4,512,512]{2,0,1:T(4,128)(2,1)S(1)}, u32[]{:S(2)}, u32[]{:S(2)}) %all-to-all-start) | async-done | bytes 2097184 | tf_op jit(solution)/shard_map/all_to_all | solution.py:100
  45.5 0.8 fusion.133
  46.4 0.5 add_reduce_fusion.1
  46.8 0.9 multiply_reduce_fusion.3
  47.8 0.7 copy.82
  48.6 0.0 copy-start.13
  48.6 2.0 copy-done.1
  50.5 1.2 fusion.39
  51.7 0.0 copy-start.5
  51.7 1.3 copy-done.5
  53.0 1.2 convolution_convert_fusion.4
  54.3 3.6 %reshape.651 = bf16[32,64,8,64]{3,2,1,0:T(8,128)(2,1)} reshape(bf16[2048,512]{1,0:T(8,128)(2,1)S(1)} %convolution_convert_fusion.4) | data formatting | bytes 4194304 | tf_op jit(solution)/shard_map/reshape | solution.py:41
  57.9 2.8 convolution_convert_fusion.3
  60.8 3.7 %reshape.652 = bf16[32,64,8,64]{3,2,1,0:T(8,128)(2,1)} reshape(bf16[2048,512]{1,0:T(8,128)(2,1)S(1)} %convolution_convert_fusion.3) | data formatting | bytes 4194304 | tf_op jit(solution)/shard_map/reshape | solution.py:46
  64.4 2.8 convolution_convert_fusion.5
  67.3 3.9 %reshape.650 = bf16[32,64,8,64]{3,2,1,0:T(8,128)(2,1)} reshape(bf16[2048,512]{1,0:T(8,128)(2,1)S(1)} %convolution_convert_fusion.5) | data formatting | bytes 4194304 | tf_op jit(solution)/shard_map/reshape | solution.py:51
  71.2 8.8 %fusion.45 = f32[64,8,32,32]{2,3,1,0:T(8,128)S(1)} fusion(bf16[32,64,8,64]{3,2,1,0:T(8,128)(2,1)} %reshape.652, bf16[32,64,8,64]{3,2,1,0:T(8,128)(2,1)} %reshape.651), kind=kOutput, calls=%fused_computation.67 | convolution fusion | flops 67108864 | bytes 6291456 | tf_op jit(solution)/shard_map/tvhd,jvhd->vhtj/dot_general | solution.py:53
  80.0 5.3 %fusion.135 = (f32[64,8,32]{2,1,0:T(8,128)S(1)}, f32[64,8,32,32]{2,3,1,0:T(8,128)}) fusion(f32[64,8,32,32]{2,3,1,0:T(8,128)S(1)} %fusion.45, pred[64,32,32]{1,2,0:T(8,128)(4,1)S(1)} %or_and_fusion), kind=kOutput, calls=%fused_computation.164 | output fusion | flops 3145759 | bytes 4325376 | tf_op jit(solution)/shard_map/sub | solution.py:62
  85.4 9.1 %convert_bitcast_fusion.3 = bf16[32,64,8,64]{3,0,2,1:T(8,128)(2,1)} fusion(f32[64,8,32,32]{2,3,1,0:T(8,128)} %get-tuple-element.14, f32[64,8,32]{2,1,0:T(8,128)S(1)} %get-tuple-element.13, bf16[32,64,8,64]{3,2,1,0:T(8,128)(2,1)S(1)} %copy-done.4), kind=kOutput, calls=%fused_computation.79 | convolution fusion | flops 69206016 | bytes 6356992 | tf_op jit(solution)/shard_map/vhtj,jvhd->tvhd/dot_general | solution.py:63
  94.5 5.7 %copy.91 = bf16[32,64,8,64]{3,2,1,0:T(8,128)(2,1)} copy(bf16[32,64,8,64]{3,0,2,1:T(8,128)(2,1)} %convert_bitcast_fusion.3) | data formatting | bytes 4194304 | tf_op jit(solution)/shard_map/convert_element_type | solution.py:66
  100.3 5.5 %reshape.653 = bf16[2048,512]{1,0:T(8,128)(2,1)S(1)} reshape(bf16[32,64,8,64]{3,2,1,0:T(8,128)(2,1)} %copy.91) | data formatting | bytes 4194304 | tf_op jit(solution)/shard_map/reshape | solution.py:66
  105.7 3.6 %fusion.136 = (f32[2048]{0:T(1024)S(1)}, f32[2048,512]{1,0:T(8,128)S(1)}) fusion(bf16[2048,512]{1,0:T(8,128)(2,1)S(1)} %reshape.653, bf16[2,512,512]{2,1,0:T(8,128)(2,1)S(1)} %copy-done.6, f32[32,512]{1,0:T(8,128)S(1)} %convert_element_type.223, f32[8,4,64,512]{3,2,1,0:T(8,128)} %copy-done.1), kind=kOutput, calls=%fused_computation.165 | convolution fusion | flops 1076885504 | bytes 11083776 | tf_op jit(solution)/shard_map/dot_general | solution.py:67
  109.4 1.9 copy-done.3
  111.3 0.8 multiply_reduce_fusion.2
  112.1 0.6 add_rsqrt_fusion.3
  112.8 8.4 %add_convert_fusion.1 = bf16[2048,512]{1,0:T(8,128)(2,1)S(1)} fusion(f32[2048,512]{1,0:T(8,128)} %copy-done.3, f32[512]{0:T(512)} %bitcast.163, f32[2048]{0:T(1024)} %add_rsqrt_fusion.3, f32[2048]{0:T(1024)S(1)} %broadcast_multiply_fusion.3, bf16[2,1024,512]{2,1,0:T(8,128)(2,1)} %param.22, bf16[2,512,1024]{2,1,0:T(8,128)(2,1)} %param.21), kind=kOutput, calls=%fused_computation.76 | convolution fusion | flops 4320133120 | bytes 12601344 | tf_op jit(solution)/shard_map/dot_general | solution.py:72
  121.1 29.2 %all_to_all.54 = bf16[32,64,512]{2,1,0:T(8,128)(2,1)S(1)} all-to-all(bf16[32,64,512]{2,1,0:T(8,128)(2,1)S(1)} %bitcast.153), channel_id=1, replica_groups=mesh['snap'=8,'clus'=4] {'snap'}, dimensions={0} | all-to-all | bytes 4194304 | tf_op jit(solution)/shard_map/all_to_all | solution.py:113
  150.4 0.2 copy.92
  150.6 7.5 %fusion.25 = bf16[4,512,512]{2,1,0:T(8,128)(2,1)} fusion(bf16[4,512,512]{2,1,0:T(8,128)(2,1)S(1)} %bitcast.155, f32[4,512]{1,0:T(4,128)S(1)} %copy-done.10, s32[4,512,512]{2,1,0:T(8,128)} %param.13, bf16[2,512,512]{2,1,0:T(8,128)(2,1)} %param.16), kind=kOutput, calls=%fused_computation.43 | convolution fusion | flops 2159017984 | bytes 13115392 | tf_op jit(solution)/shard_map/zfk,kb->zfb/dot_general | solution.py:23
  158.1 3.2 %copy.95 = bf16[4,512,512]{2,0,1:T(4,128)(2,1)S(1)} copy(bf16[4,512,512]{2,1,0:T(8,128)(2,1)} %fusion.25) | data formatting | bytes 4194304 | tf_op jit(solution)/shard_map/convert_element_type | solution.py:25
  161.3 29.3 %all_to_all.55 = bf16[4,512,512]{2,0,1:T(4,128)(2,1)S(1)} all-to-all(bf16[4,512,512]{2,0,1:T(4,128)(2,1)S(1)} %copy.95), channel_id=1, replica_groups=mesh['snap'=8,'clus'=4] {'snap'}, dimensions={1} | all-to-all | bytes 4194304 | tf_op jit(solution)/shard_map/all_to_all | solution.py:100
  190.5 0.8 fusion.132
  191.3 0.5 add_reduce_fusion
  191.8 1.0 multiply_reduce_fusion.1
  192.8 0.7 copy.97
  193.6 1.2 fusion.35
  194.8 0.8 copy-done.14
  195.5 2.6 convolution_convert_fusion.1
  198.1 2.6 convolution_convert_fusion
  200.7 1.2 convolution_convert_fusion.2
  201.9 6.2 %reshape.656 = bf16[32,64,8,64]{3,2,1,0:T(8,128)(2,1)} reshape(bf16[2048,512]{1,0:T(8,128)(2,1)} %convolution_convert_fusion.1) | data formatting | bytes 4194304 | tf_op jit(solution)/shard_map/reshape | solution.py:41
  208.1 6.4 %reshape.657 = bf16[32,64,8,64]{3,2,1,0:T(8,128)(2,1)} reshape(bf16[2048,512]{1,0:T(8,128)(2,1)} %convolution_convert_fusion) | data formatting | bytes 4194304 | tf_op jit(solution)/shard_map/reshape | solution.py:46
  214.5 8.8 %fusion.41 = f32[64,8,32,32]{2,3,1,0:T(8,128)S(1)} fusion(bf16[32,64,8,64]{3,2,1,0:T(8,128)(2,1)} %reshape.657, bf16[32,64,8,64]{3,2,1,0:T(8,128)(2,1)} %reshape.656), kind=kOutput, calls=%fused_computation.63 | convolution fusion | flops 67108864 | bytes 6291456 | tf_op jit(solution)/shard_map/tvhd,jvhd->vhtj/dot_general | solution.py:53
  223.4 5.6 %fusion.137 = (f32[64,8,32]{2,1,0:T(8,128)}, f32[64,8,32,32]{2,3,1,0:T(8,128)}) fusion(f32[64,8,32,32]{2,3,1,0:T(8,128)S(1)} %fusion.41, pred[64,32,32]{1,2,0:T(8,128)(4,1)S(1)} %or_and_fusion), kind=kOutput, calls=%fused_computation.166 | output fusion | flops 3145759 | bytes 4325376 | tf_op jit(solution)/shard_map/sub | solution.py:62
  229.0 3.9 %reshape.655 = bf16[32,64,8,64]{3,2,1,0:T(8,128)(2,1)} reshape(bf16[2048,512]{1,0:T(8,128)(2,1)S(1)} %convolution_convert_fusion.2) | data formatting | bytes 4194304 | tf_op jit(solution)/shard_map/reshape | solution.py:51
  232.9 8.1 %convert_bitcast_fusion.2 = bf16[32,64,8,64]{3,0,2,1:T(8,128)(2,1)S(1)} fusion(f32[64,8,32,32]{2,3,1,0:T(8,128)} %get-tuple-element.18, f32[64,8,32]{2,1,0:T(8,128)S(1)} %copy-done.19, bf16[32,64,8,64]{3,2,1,0:T(8,128)(2,1)} %reshape.655), kind=kOutput, calls=%fused_computation.73 | convolution fusion | flops 69206016 | bytes 6356992 | tf_op jit(solution)/shard_map/vhtj,jvhd->tvhd/dot_general | solution.py:63
  241.1 3.6 %copy.105 = bf16[32,64,8,64]{3,2,1,0:T(8,128)(2,1)} copy(bf16[32,64,8,64]{3,0,2,1:T(8,128)(2,1)S(1)} %convert_bitcast_fusion.2) | data formatting | bytes 4194304 | tf_op jit(solution)/shard_map/convert_element_type | solution.py:66
  244.6 5.4 %reshape.658 = bf16[2048,512]{1,0:T(8,128)(2,1)S(1)} reshape(bf16[32,64,8,64]{3,2,1,0:T(8,128)(2,1)} %copy.105) | data formatting | bytes 4194304 | tf_op jit(solution)/shard_map/reshape | solution.py:66
  250.0 3.6 %fusion.138 = (f32[2048]{0:T(1024)S(1)}, f32[2048,512]{1,0:T(8,128)S(1)}) fusion(bf16[2048,512]{1,0:T(8,128)(2,1)S(1)} %reshape.658, bf16[2,512,512]{2,1,0:T(8,128)(2,1)S(1)} %copy-done.6, f32[32,512]{1,0:T(8,128)S(1)} %convert_element_type.223, f32[8,4,64,512]{3,2,1,0:T(8,128)} %copy-done), kind=kOutput, calls=%fused_computation.167 | convolution fusion | flops 1076885504 | bytes 11083776 | tf_op jit(solution)/shard_map/dot_general | solution.py:67
  253.6 1.9 copy-done.2
  255.6 0.8 multiply_reduce_fusion
  256.4 8.4 %add_convert_fusion = bf16[2048,512]{1,0:T(8,128)(2,1)S(1)} fusion(f32[2048,512]{1,0:T(8,128)} %copy-done.2, f32[512]{0:T(512)S(1)} %bitcast.162, f32[2048]{0:T(1024)S(1)} %add_rsqrt_fusion.2, f32[2048]{0:T(1024)S(1)} %broadcast_multiply_fusion.2, bf16[2,1024,512]{2,1,0:T(8,128)(2,1)} %param.22, bf16[2,512,1024]{2,1,0:T(8,128)(2,1)} %param.21), kind=kOutput, calls=%fused_computation.70 | convolution fusion | flops 4320133120 | bytes 12601344 | tf_op jit(solution)/shard_map/dot_general | solution.py:72
  264.8 29.0 %all_to_all.56 = bf16[32,64,512]{2,1,0:T(8,128)(2,1)S(1)} all-to-all(bf16[32,64,512]{2,1,0:T(8,128)(2,1)S(1)} %bitcast.154), channel_id=1, replica_groups=mesh['snap'=8,'clus'=4] {'snap'}, dimensions={0} | all-to-all | bytes 4194304 | tf_op jit(solution)/shard_map/all_to_all | solution.py:113
  293.8 1.5 copy.106
  (46 shorter events, 0.2 us)
Async XLA Ops:
  0.0 2.6 copy-start.12
  2.7 7.9 %copy-start.9 = (f32[4,512]{1,0:T(4,128)}, f32[4,512]{1,0:T(4,128)S(1)}, u32[]{:S(2)}) copy-start(f32[4,512]{1,0:T(4,128)S(1)} %convert_add_fusion.4) | copy-start | bytes 24580
  10.5 8.4 %copy-start.7 = (bf16[32,512]{1,0:T(8,128)(2,1)S(1)}, bf16[32,512]{1,0:T(8,128)(2,1)}, u32[]{:S(2)}) copy-start(bf16[32,512]{1,0:T(8,128)(2,1)} %param.15) | copy-start | bytes 98308
  10.6 8.5 %copy-start.11 = (s32[64]{0:T(128)S(1)}, s32[64]{0:T(128)}, u32[]{:S(2)}) copy-start(s32[64]{0:T(128)} %param.14) | copy-start | bytes 772
  10.6 8.6 %copy-start.8 = (f32[2,2,512]{2,1,0:T(2,128)S(1)}, f32[2,2,512]{2,1,0:T(2,128)}, u32[]{:S(2)}) copy-start(f32[2,2,512]{2,1,0:T(2,128)} %param.23) | copy-start | bytes 24580
  13.5 32.0 %all-to-all-start = ((bf16[4,512,512]{2,0,1:T(4,128)(2,1)}), bf16[4,512,512]{2,0,1:T(4,128)(2,1)S(1)}, u32[]{:S(2)}, u32[]{:S(2)}) async-start(bf16[4,512,512]{2,0,1:T(4,128)(2,1)} %copy.80), calls=%async_computation | async-start | bytes 4194304 | tf_op jit(solution)/shard_map/all_to_all | solution.py:100
  48.5 2.0 copy-start.1
  48.6 4.5 %copy-start.13 = (bf16[2,512,512]{2,1,0:T(8,128)(2,1)S(1)}, bf16[2,512,512]{2,1,0:T(8,128)(2,1)}, u32[]{:S(2)}) copy-start(bf16[2,512,512]{2,1,0:T(8,128)(2,1)} %param.17) | copy-start | bytes 3145732
  51.7 1.3 copy-start.5
  54.3 3.6 %copy-start.15 = (bf16[2,512,512]{2,1,0:T(8,128)(2,1)S(1)}, bf16[2,512,512]{2,1,0:T(8,128)(2,1)}, u32[]{:S(2)}) copy-start(bf16[2,512,512]{2,1,0:T(8,128)(2,1)} %param.18) | copy-start | bytes 3145732
  60.8 3.7 %copy-start.17 = (bf16[2,512,512]{2,1,0:T(8,128)(2,1)S(1)}, bf16[2,512,512]{2,1,0:T(8,128)(2,1)}, u32[]{:S(2)}) copy-start(bf16[2,512,512]{2,1,0:T(8,128)(2,1)} %param.19) | copy-start | bytes 3145732
  80.0 5.4 %copy-start.4 = (bf16[32,64,8,64]{3,2,1,0:T(8,128)(2,1)S(1)}, bf16[32,64,8,64]{3,2,1,0:T(8,128)(2,1)}, u32[]{:S(2)}) copy-start(bf16[32,64,8,64]{3,2,1,0:T(8,128)(2,1)} %reshape.650) | copy-start | bytes 6291460
  100.3 5.5 %copy-start.6 = (bf16[2,512,512]{2,1,0:T(8,128)(2,1)S(1)}, bf16[2,512,512]{2,1,0:T(8,128)(2,1)}, u32[]{:S(2)}) copy-start(bf16[2,512,512]{2,1,0:T(8,128)(2,1)} %param.20) | copy-start | bytes 3145732
  109.4 1.9 copy-start.3
  121.1 29.5 %copy-start.10 = (f32[4,512]{1,0:T(4,128)S(1)}, f32[4,512]{1,0:T(4,128)}, u32[]{:S(2)}) copy-start(f32[4,512]{1,0:T(4,128)} %copy-done.9) | copy-start | bytes 24580
  193.5 4.6 %copy-start = (f32[8,4,64,512]{3,2,1,0:T(8,128)}, f32[8,4,64,512]{3,2,1,0:T(8,128)S(1)}, u32[]{:S(2)}) copy-start(f32[8,4,64,512]{3,2,1,0:T(8,128)S(1)} %copy.97) | copy-start | bytes 12582916
  193.6 2.0 copy-start.14
  195.5 2.6 copy-start.16
  198.1 2.6 copy-start.18
  229.0 4.0 %copy-start.19 = (f32[64,8,32]{2,1,0:T(8,128)S(1)}, f32[64,8,32]{2,1,0:T(8,128)}, u32[]{:S(2)}) copy-start(f32[64,8,32]{2,1,0:T(8,128)} %get-tuple-element.17) | copy-start | bytes 196612
  253.6 1.9 copy-start.2
where the time goes:
time: 301 us; the launch traced here: 296 us
  matrix products  87.5 us (29%)
  blocking collectives  87.5 us (29%)
  local copies, waits for them, and re-layouts  65.8 us (22%)
  waiting for transfers between devices  25.5 us (8%)
  other arithmetic  23.2 us (8%)
  starting transfers between devices  5.41 us (2%)
    all_to_all x2, blocking collectives, on_device(): lax.all_to_all(finished, 'snap', split_axis=0, concat_axis=1, tiled=True)  58.3 us
    all_to_all x1, blocking collectives, on_device(): lax.all_to_all(convolved, 'snap', split_axis=1, concat_axis=0, tiled=True)  29.3 us
    all_to_all x1, waiting for transfers between devices, on_device(): lax.all_to_all(convolved, 'snap', split_axis=1, concat_axis=0, tiled=True)  25.5 us
    dot_general x2, matrix products, temporal(): jnp.einsum('tvhd,jvhd->vhtj', queries, key_rows, preferred_element_type=j...  17.6 us
    dot_general x2, matrix products, temporal(): jnp.einsum('vhtj,jvhd->tvhd', weights, values, preferred_element_type=jnp...  17.3 us
    dot_general x2, matrix products, temporal(): jnp.dot(inner_rows, w_down, preferred_element_type=jnp.float32)  16.7 us
    dot_general x2, matrix products, convolve(): jnp.einsum('zfk,kb->zfb', blended_values, weight_matrix, preferred_elemen...  15.3 us
    sub x2, other arithmetic, temporal(): weights = jax.nn.softmax(scores, axis=-1).astype(jnp.bfloat16)  10.9 us
  transfers between devices with their start and end apart: 1, of which 1 were waited for; matrix products, arithmetic and copies ran while one was open for 0% of the time, Pallas kernels for 0%

commit v1 on v0

v1 whole, which is shorter than its diff:
```python
import functools

import jax
import jax.numpy as jnp
from jax import lax
from jax.experimental import pallas as pl
from jax.experimental.pallas import tpu as pltpu
from jax.sharding import PartitionSpec as P

HEADS = 8
LANES = 128
CHUNK = 16
GROUP = 8
F32 = jnp.float32
BF16 = jnp.bfloat16


def layer_norm(values_in, gain):
    average = jnp.mean(values_in, axis=-1, keepdims=True)
    centred = values_in - average
    scattered_rows = jnp.mean(centred * centred, axis=-1, keepdims=True)
    return centred * lax.rsqrt(scattered_rows + 1e-05) * gain


def matmul(left, right):
    return jnp.dot(left, right, preferred_element_type=F32)


def gelu(x):
    return 0.5 * x * (1.0 + jnp.tanh(0.7978845608028654 * (x + 0.044715 * (x * x * x))))


def kernel(
    n,
    features_ref,
    adjacency_ref,
    first_seen_ref,
    pos_ref,
    w_struct_ref,
    w_query_ref,
    w_key_ref,
    w_value_ref,
    w_out_ref,
    w_up_ref,
    w_down_ref,
    gain_ref,
    out_ref,
    hidden,
    adjacent,
    conv,
    arrived,
    finished,
    ws,
    wqkv,
    wo,
    wu,
    wd,
    pos,
    qkv,
    heads_out,
    in_sems,
    go_send,
    go_recv,
    back_send,
    back_recv,
    out_sem,
):
    me = lax.axis_index("snap")
    blocks = ws.shape[0]
    _, local, _, owned, width = hidden.shape
    steps = pos.shape[0]
    nodes = n * owned
    chunks = owned // CHUNK
    head_dim = width // HEADS
    rows = steps * GROUP
    groups = CHUNK // GROUP

    moves = [
        (features_ref, hidden.at[0]),
        (adjacency_ref, adjacent),
        (w_struct_ref, ws),
        (w_query_ref, wqkv.at[:, :, pl.ds(0, width)]),
        (w_key_ref, wqkv.at[:, :, pl.ds(width, width)]),
        (w_value_ref, wqkv.at[:, :, pl.ds(2 * width, width)]),
        (w_out_ref, wo),
        (w_up_ref, wu),
        (w_down_ref, wd),
    ]
    loads = [
        pltpu.make_async_copy(src, dst, in_sems.at[i]) for i, (src, dst) in enumerate(moves)
    ]
    for load in loads:
        load.start()

    barrier = pltpu.get_barrier_semaphore()

    @pl.loop(1, n)
    def _(k):
        pl.semaphore_signal(
            barrier,
            inc=1,
            device_id={"snap": lax.rem(me + k, n)},
            device_id_type=pl.DeviceIdType.MESH,
        )

    pos[...] = jnp.broadcast_to(
        pos_ref[...].astype(F32)[:, None, :], (steps, GROUP, width)
    )
    pl.semaphore_wait(barrier, n - 1)

    def go(b, c, peer, sender):
        return pltpu.make_async_remote_copy(
            src_ref=conv.at[b, c, peer],
            dst_ref=arrived.at[b, c, pl.ds(sender * local, local)],
            send_sem=go_send.at[b, c, peer],
            recv_sem=go_recv.at[b, c, sender],
            device_id={"snap": peer},
            device_id_type=pl.DeviceIdType.MESH,
        )

    def back(b, c, peer, sender):
        return pltpu.make_async_remote_copy(
            src_ref=finished.at[b, c, pl.ds(peer * local, local)],
            dst_ref=hidden.at[b + 1, :, sender, pl.ds(c * CHUNK, CHUNK)],
            send_sem=back_send.at[b, c, peer],
            recv_sem=back_recv.at[b, c, sender],
            device_id={"snap": peer},
            device_id_type=pl.DeviceIdType.MESH,
        )

    def convolve(b, c):
        mine = pl.ds(c * CHUNK, CHUNK)
        blended, own_rows = [], []
        for s in range(local):
            links = adjacent[s, :, mine, :].reshape(n * CHUNK, nodes).astype(F32)
            degree = 1.0 + jnp.sum(links, axis=-1, keepdims=True)
            own = hidden[b, s, :, mine, :].reshape(n * CHUNK, width).astype(F32)
            summed = matmul(links.astype(BF16), hidden[b, s].reshape(nodes, width)) + own
            blended.append((summed / degree).astype(BF16))
            own_rows.append(own)
        projected = matmul(jnp.concatenate(blended, axis=0), ws[b])
        projected = jnp.where(projected > 0, projected, jnp.exp(jnp.minimum(projected, 0.0)) - 1.0)
        result = (projected + jnp.concatenate(own_rows, axis=0)).astype(BF16)
        result = result.reshape(local, n, CHUNK, width)
        for s in range(local):
            conv[b, c, :, s] = result[s]

    def attend(c, g):
        base = g * rows
        lane = lax.broadcasted_iota(jnp.int32, (1, rows), 1)
        seen = jnp.zeros((1, rows), jnp.int32)
        for i in range(GROUP):
            seen = jnp.where(
                lane % GROUP == i, first_seen_ref[c * CHUNK + g * GROUP + i], seen
            )
        row_at = lax.broadcasted_iota(jnp.int32, (rows, rows), 0)
        col_at = lax.broadcasted_iota(jnp.int32, (rows, rows), 1)
        t, j = row_at // GROUP, col_at // GROUP
        allowed = (row_at % GROUP == col_at % GROUP) & (j <= t) & ((j >= seen) | (j == t))
        bias = jnp.where(allowed, 0.0, -1e30)
        tile_lane = lax.broadcasted_iota(jnp.int32, (1, LANES), 1)
        for tile in range(width // LANES):
            q = qkv[pl.ds(base, rows), pl.ds(tile * LANES, LANES)]
            k = qkv[pl.ds(base, rows), pl.ds(width + tile * LANES, LANES)]
            v = qkv[pl.ds(base, rows), pl.ds(2 * width + tile * LANES, LANES)]
            total = jnp.zeros((rows, 2 * LANES), F32)
            for h in range(LANES // head_dim):
                chosen = jnp.where(tile_lane // head_dim == h, 1.0, 0.0).astype(BF16)
                scores = lax.dot_general(
                    q, k * chosen, (((1,), (1,)), ((), ())), preferred_element_type=F32
                )
                scores = scores + bias
                top = jnp.max(scores, axis=-1, keepdims=True)
                weights = jnp.exp(scores - top).astype(BF16)
                wide = jnp.concatenate(
                    [v * chosen, jnp.broadcast_to(chosen, (rows, LANES))], axis=1
                )
                total = total + matmul(weights, wide)
            heads_out[pl.ds(base, rows), pl.ds(tile * LANES, LANES)] = (
                total[:, :LANES] / total[:, LANES:]
            ).astype(BF16)

    def temporal(b, c):
        arrivals = arrived[b, c].astype(F32)
        summed = jnp.concatenate(
            [
                (arrivals[:, g * GROUP : (g + 1) * GROUP, :] + pos[...]).reshape(rows, width)
                for g in range(groups)
            ],
            axis=0,
        )
        normed = layer_norm(summed, gain_ref[b, pl.ds(0, 1), :]).astype(BF16)
        qkv[:, pl.ds(0, width)] = (
            matmul(normed, wqkv[b, :, pl.ds(0, width)]) * head_dim ** (-0.5)
        ).astype(BF16)
        qkv[:, pl.ds(width, 2 * width)] = matmul(
            normed, wqkv[b, :, pl.ds(width, 2 * width)]
        ).astype(BF16)
        for g in range(groups):
            attend(c, g)
        attended = summed + matmul(heads_out[...], wo[b])
        normed_two = layer_norm(attended, gain_ref[b, pl.ds(1, 1), :]).astype(BF16)
        inner = gelu(matmul(normed_two, wu[b])).astype(BF16)
        result = attended + matmul(inner, wd[b])
        finished[b, c] = jnp.concatenate(
            [
                result[g * rows : (g + 1) * rows].reshape(steps, GROUP, width)
                for g in range(groups)
            ],
            axis=1,
        ).astype(BF16)

    for load in loads:
        load.wait()

    @pl.loop(0, blocks)
    def _(b):
        @pl.loop(0, chunks)
        def _(c):
            convolve(b, c)

            @pl.loop(1, n)
            def _(k):
                go(b, c, lax.rem(me + k, n), me).start()

            arrived[b, c, pl.ds(me * local, local)] = conv[b, c, me]

        @pl.loop(0, chunks)
        def _(c):
            @pl.loop(1, n)
            def _(k):
                peer = lax.rem(me + k, n)
                go(b, c, peer, peer).wait_recv()

            temporal(b, c)

            @pl.loop(1, n)
            def _(k):
                back(b, c, lax.rem(me + k, n), me).start()

            hidden[b + 1, :, me, pl.ds(c * CHUNK, CHUNK), :] = finished[
                b, c, pl.ds(me * local, local)
            ]

        @pl.loop(0, chunks)
        def _(c):
            @pl.loop(1, n)
            def _(k):
                peer = lax.rem(me + k, n)
                back(b, c, peer, peer).wait_recv()

    store = pltpu.make_async_copy(hidden.at[blocks], out_ref, out_sem)
    store.start()

    @pl.loop(0, blocks)
    def _(b):
        @pl.loop(0, chunks)
        def _(c):
            @pl.loop(1, n)
            def _(k):
                peer = lax.rem(me + k, n)
                go(b, c, peer, me).wait_send()
                back(b, c, peer, me).wait_send()

    store.wait()


def on_device(n, features, adjacency, first_seen, pos_embed, *weights):
    local, nodes, width = features.shape
    blocks, _, hidden_units = weights[5].shape
    owned = nodes // n
    chunks = owned // CHUNK
    steps = pos_embed.shape[0]
    chunk_rows = steps * CHUNK
    anywhere = pl.BlockSpec(memory_space=pl.ANY)
    in_vmem = pl.BlockSpec(memory_space=pltpu.VMEM)
    result = pl.pallas_call(
        functools.partial(kernel, n),
        out_shape=jax.ShapeDtypeStruct((local, n, owned, width), BF16),
        in_specs=[
            anywhere,
            anywhere,
            pl.BlockSpec(memory_space=pltpu.SMEM),
            in_vmem,
            *[anywhere] * 7,
            in_vmem,
        ],
        out_specs=anywhere,
        scratch_shapes=[
            pltpu.VMEM((blocks + 1, local, n, owned, width), BF16),
            pltpu.VMEM((local, n, owned, nodes), jnp.int32),
            pltpu.VMEM((blocks, chunks, n, local, CHUNK, width), BF16),
            pltpu.VMEM((blocks, chunks, steps, CHUNK, width), BF16),
            pltpu.VMEM((blocks, chunks, steps, CHUNK, width), BF16),
            pltpu.VMEM((blocks, width, width), BF16),
            pltpu.VMEM((blocks, width, 3 * width), BF16),
            pltpu.VMEM((blocks, width, width), BF16),
            pltpu.VMEM((blocks, width, hidden_units), BF16),
            pltpu.VMEM((blocks, hidden_units, width), BF16),
            pltpu.VMEM((steps, GROUP, width), F32),
            pltpu.VMEM((chunk_rows, 3 * width), BF16),
            pltpu.VMEM((chunk_rows, width), BF16),
            pltpu.SemaphoreType.DMA((9,)),
            pltpu.SemaphoreType.DMA((blocks, chunks, n)),
            pltpu.SemaphoreType.DMA((blocks, chunks, n)),
            pltpu.SemaphoreType.DMA((blocks, chunks, n)),
            pltpu.SemaphoreType.DMA((blocks, chunks, n)),
            pltpu.SemaphoreType.DMA,
        ],
        compiler_params=pltpu.CompilerParams(
            collective_id=0, has_side_effects=True, vmem_limit_bytes=56 * 2**20
        ),
    )(
        features.reshape(local, n, owned, width),
        adjacency.reshape(local, n, owned, nodes),
        first_seen,
        pos_embed,
        *weights,
    )
    return result.reshape(local, nodes, width)


def solution(mesh):
    in_specs = (
        P("snap", "clus", None),
        P("snap", "clus", None),
        P(("clus", "snap")),
        *[P()] * 9,
    )
    return jax.shard_map(
        functools.partial(on_device, mesh.shape["snap"]),
        mesh=mesh,
        in_specs=in_specs,
        out_specs=P("snap", "clus", None),
        check_vma=False,
    )
```

time: 301 us -> 111 us (0.37); the launches traced: 296 us -> 110 us
  Pallas kernels: 0 us -> 107 us
  matrix products: 87.5 us -> 0 us
  blocking collectives: 87.5 us -> 0 us
  local copies, waits for them, and re-layouts: 65.8 us -> 3.05 us
  waiting for transfers between devices: 25.5 us -> 0 us
  other arithmetic: 23.2 us -> 0 us
  starting transfers between devices: 5.41 us -> 0 us
    pallas_call x0 -> x1, Pallas kernels: none -> 107 us  [on_device(): pl.pallas_call(functools.partial(kernel, n), out_shape=jax.ShapeDtypeStru...]
    all_to_all x3 -> x0, blocking collectives: 87.5 us -> none  [the longest x2 58.3 us: on_device(): lax.all_to_all(finished, 'snap', split_axis=0, concat_axis=1, tiled=True)]
    dot_general x16 -> x0, matrix products: 87.5 us -> none  [the longest x2 17.6 us: temporal(): jnp.einsum('tvhd,jvhd->vhtj', queries, key_rows, preferred_element_type=j...]
    reshape x8 -> x0, local copies, waits for them, and re-layouts: 38.6 us -> none  [the longest x2 10.8 us: temporal(): attended_heads.astype(jnp.bfloat16).reshape(-1, model_width)]
    all_to_all x1 -> x0, waiting for transfers between devices: 25.5 us -> none  [on_device(): lax.all_to_all(convolved, 'snap', split_axis=1, concat_axis=0, tiled=True)]
    convert_element_type x6 -> x0, local copies, waits for them, and re-layouts: 16.8 us -> none  [the longest x2 9.29 us: temporal(): attended_heads.astype(jnp.bfloat16).reshape(-1, model_width)]
    sub x2 -> x0, other arithmetic: 10.9 us -> none  [temporal(): weights = jax.nn.softmax(scores, axis=-1).astype(jnp.bfloat16)]
    reduce_sum x7 -> x0, other arithmetic: 7.16 us -> none  [the longest x4 3.59 us: layer_norm(): scattered_rows = jnp.mean(centred * centred, axis=-1, keepdims=True)]
  transfers between devices with their start and end apart: 1 -> 0, of which waited for: 1 -> 0; matrix products, arithmetic and copies ran while one was open for 0% -> 0% of each run, Pallas kernels for 0% -> 0%
where the time goes in v1:
time: 111 us; the launch traced here: 110 us
  Pallas kernels  107 us (96%)
  local copies, waits for them, and re-layouts  3.05 us (3%)
    pallas_call x1, Pallas kernels, on_device(): pl.pallas_call(functools.partial(kernel, n), out_shape=jax.ShapeDtypeStru...  107 us
    unnamed x1, local copies, waits for them, and re-layouts  3.05 us

profile of v1, /device:TPU:0, one launch (start us, length us, event | category | flops | bytes accessed | tf_op | source)
XLA Modules:
  0.0 109.9 jit_solution(8488838975622243019)
XLA Ops:
  0.0 106.9 %shard_map.118 = bf16[4,8,64,512]{3,2,1,0:T(8,128)(2,1)} custom-call(bf16[4,8,64,512]{3,2,1,0:T(8,128)(2,1)} %bitcast.5, s32[4,8,64,512]{3,2,1,0:T(8,128)} %bitcast.4, s32[64]{0:T(128)} %first_seen_ref.1, bf16[32,512]{1,0:T(8,128)(2,1)} %pos_ref.1, bf16[2,512,512]{2,1,0:T(8,128)(2,1)} %w_struct_ref.1, bf16[2,512,512]{2,1,0:T(8,128)(2,1)} %w_query_ref.1, ...), custom_call_target="tpu_custom_call" | custom-call | tf_op jit(solution)/shard_map/pallas_call | solution.py:277
  106.9 3.0 %copy.14 = bf16[4,512,512]{2,1,0:T(8,128)(2,1)} copy(bf16[4,512,512]{2,1,0:T(8,128)(2,1)} %bitcast.3) | data formatting | bytes 4194304

commit v2 on v1

--- a/solution.py
+++ b/solution.py
@@ -11,6 +11,7 @@
 LANES = 128
 CHUNK = 16
 GROUP = 8
+SPANS = 2
 F32 = jnp.float32
 BF16 = jnp.bfloat16
 
@@ -27,7 +28,8 @@
 
 
 def gelu(x):
-    return 0.5 * x * (1.0 + jnp.tanh(0.7978845608028654 * (x + 0.044715 * (x * x * x))))
+    half = 0.5 * x
+    return half + half * jnp.tanh(x * (0.7978845608028654 + 0.035677408136300125 * (x * x)))
 
 
 def kernel(
@@ -59,6 +61,7 @@
     qkv,
     heads_out,
     in_sems,
+    link_sems,
     go_send,
     go_recv,
     back_send,
@@ -75,9 +78,14 @@
     rows = steps * GROUP
     groups = CHUNK // GROUP
 
+    def load_links(c):
+        part = pl.ds(c * CHUNK, CHUNK)
+        return pltpu.make_async_copy(
+            adjacency_ref.at[:, :, part], adjacent.at[:, :, part], link_sems.at[c]
+        )
+
     moves = [
         (features_ref, hidden.at[0]),
-        (adjacency_ref, adjacent),
         (w_struct_ref, ws),
         (w_query_ref, wqkv.at[:, :, pl.ds(0, width)]),
         (w_key_ref, wqkv.at[:, :, pl.ds(width, width)]),
@@ -89,44 +97,69 @@
     loads = [
         pltpu.make_async_copy(src, dst, in_sems.at[i]) for i, (src, dst) in enumerate(moves)
     ]
-    for load in loads:
+    loads[0].start()
+    load_links(0).start()
+    loads[1].start()
+    for c in range(1, chunks):
+        load_links(c).start()
+    for load in loads[2:]:
         load.start()
 
     barrier = pltpu.get_barrier_semaphore()
-
-    @pl.loop(1, n)
-    def _(k):
+    for k in range(1, n):
         pl.semaphore_signal(
             barrier,
             inc=1,
             device_id={"snap": lax.rem(me + k, n)},
             device_id_type=pl.DeviceIdType.MESH,
         )
-
     pos[...] = jnp.broadcast_to(
         pos_ref[...].astype(F32)[:, None, :], (steps, GROUP, width)
     )
-    pl.semaphore_wait(barrier, n - 1)
-
-    def go(b, c, peer, sender):
+
+    def send(src, dst, send_sem, recv_sem, peer):
         return pltpu.make_async_remote_copy(
-            src_ref=conv.at[b, c, peer],
-            dst_ref=arrived.at[b, c, pl.ds(sender * local, local)],
-            send_sem=go_send.at[b, c, peer],
-            recv_sem=go_recv.at[b, c, sender],
+            src_ref=src,
+            dst_ref=dst,
+            send_sem=send_sem,
+            recv_sem=recv_sem,
             device_id={"snap": peer},
             device_id_type=pl.DeviceIdType.MESH,
         )
 
-    def back(b, c, peer, sender):
-        return pltpu.make_async_remote_copy(
-            src_ref=finished.at[b, c, pl.ds(peer * local, local)],
-            dst_ref=hidden.at[b + 1, :, sender, pl.ds(c * CHUNK, CHUNK)],
-            send_sem=back_send.at[b, c, peer],
-            recv_sem=back_recv.at[b, c, sender],
-            device_id={"snap": peer},
-            device_id_type=pl.DeviceIdType.MESH,
-        )
+    others = pl.ds(0, n - 1)
+
+    def go(b, c, peer):
+        return send(
+            conv.at[b, c, peer],
+            arrived.at[b, c, pl.ds(me * local, local)],
+            go_send.at[b],
+            go_recv.at[b, c],
+            peer,
+        )
+
+    def back(b, c, peer, target):
+        return send(
+            finished.at[b, c, pl.ds(peer * local, local)],
+            target.at[:, me, pl.ds(c * CHUNK, CHUNK)],
+            back_send.at[b],
+            back_recv.at[b],
+            peer,
+        )
+
+    def await_chunk(b, c):
+        view = arrived.at[b, c, pl.ds(0, (n - 1) * local)]
+        send(view, view, go_send.at[b], go_recv.at[b, c], me).wait_recv()
+
+    def await_back(b, target):
+        view = target.at[:, others]
+        send(view, view, back_send.at[b], back_recv.at[b], me).wait_recv()
+
+    def await_sent(b):
+        view = conv.at[b, :, others]
+        send(view, view, go_send.at[b], go_recv.at[b, 0], me).wait_send()
+        view = finished.at[b, :, pl.ds(0, (n - 1) * local)]
+        send(view, view, back_send.at[b], back_recv.at[b], me).wait_send()
 
     def convolve(b, c):
         mine = pl.ds(c * CHUNK, CHUNK)
@@ -136,7 +169,7 @@
             degree = 1.0 + jnp.sum(links, axis=-1, keepdims=True)
             own = hidden[b, s, :, mine, :].reshape(n * CHUNK, width).astype(F32)
             summed = matmul(links.astype(BF16), hidden[b, s].reshape(nodes, width)) + own
-            blended.append((summed / degree).astype(BF16))
+            blended.append((summed * (1.0 / degree)).astype(BF16))
             own_rows.append(own)
         projected = matmul(jnp.concatenate(blended, axis=0), ws[b])
         projected = jnp.where(projected > 0, projected, jnp.exp(jnp.minimum(projected, 0.0)) - 1.0)
@@ -163,22 +196,30 @@
             q = qkv[pl.ds(base, rows), pl.ds(tile * LANES, LANES)]
             k = qkv[pl.ds(base, rows), pl.ds(width + tile * LANES, LANES)]
             v = qkv[pl.ds(base, rows), pl.ds(2 * width + tile * LANES, LANES)]
-            total = jnp.zeros((rows, 2 * LANES), F32)
+            totals = [None] * SPANS
             for h in range(LANES // head_dim):
                 chosen = jnp.where(tile_lane // head_dim == h, 1.0, 0.0).astype(BF16)
-                scores = lax.dot_general(
-                    q, k * chosen, (((1,), (1,)), ((), ())), preferred_element_type=F32
-                )
-                scores = scores + bias
-                top = jnp.max(scores, axis=-1, keepdims=True)
-                weights = jnp.exp(scores - top).astype(BF16)
+                keys = k * chosen
                 wide = jnp.concatenate(
                     [v * chosen, jnp.broadcast_to(chosen, (rows, LANES))], axis=1
                 )
-                total = total + matmul(weights, wide)
-            heads_out[pl.ds(base, rows), pl.ds(tile * LANES, LANES)] = (
-                total[:, :LANES] / total[:, LANES:]
-            ).astype(BF16)
+                for i in range(SPANS):
+                    start, end = i * (rows // SPANS), (i + 1) * (rows // SPANS)
+                    scores = lax.dot_general(
+                        q[start:end],
+                        keys[:end],
+                        (((1,), (1,)), ((), ())),
+                        preferred_element_type=F32,
+                    )
+                    scores = scores + bias[start:end, :end]
+                    top = jnp.max(scores, axis=-1, keepdims=True)
+                    weights = jnp.exp(scores - top).astype(BF16)
+                    part = matmul(weights, wide[:end])
+                    totals[i] = part if h == 0 else totals[i] + part
+            for i, total in enumerate(totals):
+                heads_out[
+                    pl.ds(base + i * (rows // SPANS), rows // SPANS), pl.ds(tile * LANES, LANES)
+                ] = (total[:, :LANES] / total[:, LANES:]).astype(BF16)
 
     def temporal(b, c):
         arrivals = arrived[b, c].astype(F32)
@@ -210,59 +251,65 @@
             axis=1,
         ).astype(BF16)
 
-    for load in loads:
-        load.wait()
+    last = blocks - 1
+    peers = [lax.rem(me + k, n) for k in range(1, n)]
+    loads[0].wait()
+    loads[1].wait()
 
     @pl.loop(0, blocks)
     def _(b):
         @pl.loop(0, chunks)
         def _(c):
+            @pl.when(b == 0)
+            def _():
+                load_links(c).wait()
+
             convolve(b, c)
 
-            @pl.loop(1, n)
-            def _(k):
-                go(b, c, lax.rem(me + k, n), me).start()
-
+            @pl.when((b == 0) & (c == 0))
+            def _():
+                pl.semaphore_wait(barrier, n - 1)
+
+            for peer in peers:
+                go(b, c, peer).start()
             arrived[b, c, pl.ds(me * local, local)] = conv[b, c, me]
+
+        @pl.when(b == 0)
+        def _():
+            for load in loads[2:]:
+                load.wait()
 
         @pl.loop(0, chunks)
         def _(c):
-            @pl.loop(1, n)
-            def _(k):
-                peer = lax.rem(me + k, n)
-                go(b, c, peer, peer).wait_recv()
-
+            await_chunk(b, c)
             temporal(b, c)
-
-            @pl.loop(1, n)
-            def _(k):
-                back(b, c, lax.rem(me + k, n), me).start()
-
-            hidden[b + 1, :, me, pl.ds(c * CHUNK, CHUNK), :] = finished[
-                b, c, pl.ds(me * local, local)
-            ]
-
-        @pl.loop(0, chunks)
-        def _(c):
-            @pl.loop(1, n)
-            def _(k):
-                peer = lax.rem(me + k, n)
-                back(b, c, peer, peer).wait_recv()
-
-    store = pltpu.make_async_copy(hidden.at[blocks], out_ref, out_sem)
-    store.start()
-
-    @pl.loop(0, blocks)
-    def _(b):
-        @pl.loop(0, chunks)
-        def _(c):
-            @pl.loop(1, n)
-            def _(k):
-                peer = lax.rem(me + k, n)
-                go(b, c, peer, me).wait_send()
-                back(b, c, peer, me).wait_send()
-
-    store.wait()
+            part = pl.ds(c * CHUNK, CHUNK)
+            own = pl.ds(me * local, local)
+
+            @pl.when(b < last)
+            def _():
+                for peer in peers:
+                    back(b, c, peer, hidden.at[b + 1]).start()
+                hidden[b + 1, :, me, part, :] = finished[b, c, own]
+
+            @pl.when(b == last)
+            def _():
+                for peer in peers:
+                    back(b, c, peer, out_ref).start()
+                pltpu.make_async_copy(
+                    finished.at[b, c, own], out_ref.at[:, me, part], out_sem
+                ).start()
+
+        @pl.when(b < last)
+        def _():
+            await_back(b, hidden.at[b + 1])
+
+    for b in range(blocks):
+        await_sent(b)
+    await_back(last, out_ref)
+    pltpu.make_async_copy(
+        finished.at[last, :, pl.ds(0, local)], finished.at[last, :, pl.ds(0, local)], out_sem
+    ).wait()
 
 
 def on_device(n, features, adjacency, first_seen, pos_embed, *weights):
@@ -287,7 +334,7 @@
         ],
         out_specs=anywhere,
         scratch_shapes=[
-            pltpu.VMEM((blocks + 1, local, n, owned, width), BF16),
+            pltpu.VMEM((blocks, local, n, owned, width), BF16),
             pltpu.VMEM((local, n, owned, nodes), jnp.int32),
             pltpu.VMEM((blocks, chunks, n, local, CHUNK, width), BF16),
             pltpu.VMEM((blocks, chunks, steps, CHUNK, width), BF16),
@@ -300,11 +347,12 @@
             pltpu.VMEM((steps, GROUP, width), F32),
             pltpu.VMEM((chunk_rows, 3 * width), BF16),
             pltpu.VMEM((chunk_rows, width), BF16),
-            pltpu.SemaphoreType.DMA((9,)),
-            pltpu.SemaphoreType.DMA((blocks, chunks, n)),
-            pltpu.SemaphoreType.DMA((blocks, chunks, n)),
-            pltpu.SemaphoreType.DMA((blocks, chunks, n)),
-            pltpu.SemaphoreType.DMA((blocks, chunks, n)),
+            pltpu.SemaphoreType.DMA((8,)),
+            pltpu.SemaphoreType.DMA((chunks,)),
+            pltpu.SemaphoreType.DMA((blocks,)),
+            pltpu.SemaphoreType.DMA((blocks, chunks)),
+            pltpu.SemaphoreType.DMA((blocks,)),
+            pltpu.SemaphoreType.DMA((blocks,)),
             pltpu.SemaphoreType.DMA,
         ],
         compiler_params=pltpu.CompilerParams(

time: 111 us -> 105 us (0.946)
  Pallas kernels: 107 us -> 101 us
    pallas_call x1, Pallas kernels: 107 us -> 101 us  [on_device(): pl.pallas_call(functools.partial(kernel, n), out_shape=jax.ShapeDtypeStru...]
where the time goes in v2:
time: 105 us; the launch traced here: 104 us
  Pallas kernels  101 us (96%)
  local copies, waits for them, and re-layouts  3.05 us (3%)
    pallas_call x1, Pallas kernels, on_device(): pl.pallas_call(functools.partial(kernel, n), out_shape=jax.ShapeDtypeStru...  101 us
    unnamed x1, local copies, waits for them, and re-layouts  3.05 us

profile of v2, /device:TPU:0, one launch (start us, length us, event | category | flops | bytes accessed | tf_op | source)
XLA Modules:
  0.0 103.8 jit_solution(2534017237402319939)
XLA Ops:
  0.0 100.8 %shard_map.118 = bf16[4,8,64,512]{3,2,1,0:T(8,128)(2,1)} custom-call(bf16[4,8,64,512]{3,2,1,0:T(8,128)(2,1)} %bitcast.5, s32[4,8,64,512]{3,2,1,0:T(8,128)} %bitcast.4, s32[64]{0:T(128)} %first_seen_ref.1, bf16[32,512]{1,0:T(8,128)(2,1)} %pos_ref.1, bf16[2,512,512]{2,1,0:T(8,128)(2,1)} %w_struct_ref.1, bf16[2,512,512]{2,1,0:T(8,128)(2,1)} %w_query_ref.1, ...), custom_call_target="tpu_custom_call" | custom-call | tf_op jit(solution)/shard_map/pallas_call | solution.py:324
  100.8 3.0 %copy.14 = bf16[4,512,512]{2,1,0:T(8,128)(2,1)} copy(bf16[4,512,512]{2,1,0:T(8,128)(2,1)} %bitcast.3) | data formatting | bytes 4194304

commit v3 on v2

--- a/solution.py
+++ b/solution.py
@@ -12,6 +12,8 @@
 CHUNK = 16
 GROUP = 8
 SPANS = 2
+LAG = 4
+FF_TILE = 256
 F32 = jnp.float32
 BF16 = jnp.bfloat16
 
@@ -60,6 +62,8 @@
     pos,
     qkv,
     heads_out,
+    bias,
+    inner,
     in_sems,
     link_sems,
     go_send,
@@ -178,8 +182,7 @@
         for s in range(local):
             conv[b, c, :, s] = result[s]
 
-    def attend(c, g):
-        base = g * rows
+    def mask_of(c, g):
         lane = lax.broadcasted_iota(jnp.int32, (1, rows), 1)
         seen = jnp.zeros((1, rows), jnp.int32)
         for i in range(GROUP):
@@ -190,66 +193,78 @@
         col_at = lax.broadcasted_iota(jnp.int32, (rows, rows), 1)
         t, j = row_at // GROUP, col_at // GROUP
         allowed = (row_at % GROUP == col_at % GROUP) & (j <= t) & ((j >= seen) | (j == t))
-        bias = jnp.where(allowed, 0.0, -1e30)
+        bias[g] = jnp.where(allowed, 0.0, -1e30)
+
+    def attend(g, tile):
+        at = g * rows
+        span = rows // SPANS
         tile_lane = lax.broadcasted_iota(jnp.int32, (1, LANES), 1)
+        q = qkv[at : at + rows, tile * LANES : (tile + 1) * LANES]
+        k = qkv[at : at + rows, width + tile * LANES : width + (tile + 1) * LANES]
+        v = qkv[at : at + rows, 2 * width + tile * LANES : 2 * width + (tile + 1) * LANES]
+        totals = [None] * SPANS
+        for h in range(LANES // head_dim):
+            chosen = jnp.where(tile_lane // head_dim == h, 1.0, 0.0).astype(BF16)
+            keys = k * chosen
+            wide = jnp.concatenate(
+                [v * chosen, jnp.broadcast_to(chosen, (rows, LANES))], axis=1
+            )
+            for i in range(SPANS):
+                start, end = i * span, (i + 1) * span
+                scores = lax.dot_general(
+                    q[start:end],
+                    keys[:end],
+                    (((1,), (1,)), ((), ())),
+                    preferred_element_type=F32,
+                )
+                scores = scores + bias[g, start:end, :end]
+                top = jnp.max(scores, axis=-1, keepdims=True)
+                weights = jnp.exp(scores - top).astype(BF16)
+                part = matmul(weights, wide[:end])
+                totals[i] = part if h == 0 else totals[i] + part
+        for i, total in enumerate(totals):
+            heads_out[
+                at + i * span : at + (i + 1) * span, tile * LANES : (tile + 1) * LANES
+            ] = (total[:, :LANES] / total[:, LANES:]).astype(BF16)
+
+    def group_steps(b, c, g, results):
+        at = slice(g * rows, (g + 1) * rows)
+        arrivals = arrived[b, c].astype(F32)[:, g * GROUP : (g + 1) * GROUP, :]
+        summed = (arrivals + pos[...]).reshape(rows, width)
+        normed = layer_norm(summed, gain_ref[b, pl.ds(0, 1), :]).astype(BF16)
+        mask_of(c, g)
+        yield
+        qkv[at, :width] = (matmul(normed, wqkv[b, :, :width]) * head_dim ** (-0.5)).astype(BF16)
+        yield
+        qkv[at, width : 2 * width] = matmul(normed, wqkv[b, :, width : 2 * width]).astype(BF16)
+        yield
+        qkv[at, 2 * width :] = matmul(normed, wqkv[b, :, 2 * width :]).astype(BF16)
+        yield
         for tile in range(width // LANES):
-            q = qkv[pl.ds(base, rows), pl.ds(tile * LANES, LANES)]
-            k = qkv[pl.ds(base, rows), pl.ds(width + tile * LANES, LANES)]
-            v = qkv[pl.ds(base, rows), pl.ds(2 * width + tile * LANES, LANES)]
-            totals = [None] * SPANS
-            for h in range(LANES // head_dim):
-                chosen = jnp.where(tile_lane // head_dim == h, 1.0, 0.0).astype(BF16)
-                keys = k * chosen
-                wide = jnp.concatenate(
-                    [v * chosen, jnp.broadcast_to(chosen, (rows, LANES))], axis=1
-                )
-                for i in range(SPANS):
-                    start, end = i * (rows // SPANS), (i + 1) * (rows // SPANS)
-                    scores = lax.dot_general(
-                        q[start:end],
-                        keys[:end],
-                        (((1,), (1,)), ((), ())),
-                        preferred_element_type=F32,
-                    )
-                    scores = scores + bias[start:end, :end]
-                    top = jnp.max(scores, axis=-1, keepdims=True)
-                    weights = jnp.exp(scores - top).astype(BF16)
-                    part = matmul(weights, wide[:end])
-                    totals[i] = part if h == 0 else totals[i] + part
-            for i, total in enumerate(totals):
-                heads_out[
-                    pl.ds(base + i * (rows // SPANS), rows // SPANS), pl.ds(tile * LANES, LANES)
-                ] = (total[:, :LANES] / total[:, LANES:]).astype(BF16)
+            attend(g, tile)
+            yield
+        attended = summed + matmul(heads_out[at, :], wo[b])
+        normed_two = layer_norm(attended, gain_ref[b, pl.ds(1, 1), :]).astype(BF16)
+        yield
+        hidden_units = wu.shape[2]
+        for start in range(0, hidden_units, FF_TILE):
+            part = slice(start, start + FF_TILE)
+            inner[at, part] = gelu(matmul(normed_two, wu[b, :, part])).astype(BF16)
+            yield
+        results[g] = (attended + matmul(inner[at, :], wd[b])).reshape(steps, GROUP, width)
 
     def temporal(b, c):
-        arrivals = arrived[b, c].astype(F32)
-        summed = jnp.concatenate(
-            [
-                (arrivals[:, g * GROUP : (g + 1) * GROUP, :] + pos[...]).reshape(rows, width)
-                for g in range(groups)
-            ],
-            axis=0,
-        )
-        normed = layer_norm(summed, gain_ref[b, pl.ds(0, 1), :]).astype(BF16)
-        qkv[:, pl.ds(0, width)] = (
-            matmul(normed, wqkv[b, :, pl.ds(0, width)]) * head_dim ** (-0.5)
-        ).astype(BF16)
-        qkv[:, pl.ds(width, 2 * width)] = matmul(
-            normed, wqkv[b, :, pl.ds(width, 2 * width)]
-        ).astype(BF16)
-        for g in range(groups):
-            attend(c, g)
-        attended = summed + matmul(heads_out[...], wo[b])
-        normed_two = layer_norm(attended, gain_ref[b, pl.ds(1, 1), :]).astype(BF16)
-        inner = gelu(matmul(normed_two, wu[b])).astype(BF16)
-        result = attended + matmul(inner, wd[b])
-        finished[b, c] = jnp.concatenate(
-            [
-                result[g * rows : (g + 1) * rows].reshape(steps, GROUP, width)
-                for g in range(groups)
-            ],
-            axis=1,
-        ).astype(BF16)
+        results = [None] * groups
+        waiting = [group_steps(b, c, g, results) for g in range(groups)]
+        running, tick = [], 0
+        while waiting or running:
+            if waiting and tick % LAG == 0:
+                running.append(waiting.pop(0))
+            for steps_left in list(running):
+                if next(steps_left, 0) == 0:
+                    running.remove(steps_left)
+            tick += 1
+        finished[b, c] = jnp.concatenate(results, axis=1).astype(BF16)
 
     last = blocks - 1
     peers = [lax.rem(me + k, n) for k in range(1, n)]
@@ -347,6 +362,8 @@
             pltpu.VMEM((steps, GROUP, width), F32),
             pltpu.VMEM((chunk_rows, 3 * width), BF16),
             pltpu.VMEM((chunk_rows, width), BF16),
+            pltpu.VMEM((CHUNK // GROUP, steps * GROUP, steps * GROUP), F32),
+            pltpu.VMEM((chunk_rows, hidden_units), BF16),
             pltpu.SemaphoreType.DMA((8,)),
             pltpu.SemaphoreType.DMA((chunks,)),
             pltpu.SemaphoreType.DMA((blocks,)),

time: 105 us -> 105 us (level)
  no operation moved by 1% of the time
where the time goes in v3:
time: 105 us; the launch traced here: 104 us
  Pallas kernels  101 us (96%)
  local copies, waits for them, and re-layouts  3.05 us (3%)
    pallas_call x1, Pallas kernels, on_device(): pl.pallas_call(functools.partial(kernel, n), out_shape=jax.ShapeDtypeStru...  101 us
    unnamed x1, local copies, waits for them, and re-layouts  3.05 us

profile of v3, /device:TPU:0, one launch (start us, length us, event | category | flops | bytes accessed | tf_op | source)
XLA Modules:
  0.0 103.8 jit_solution(10267750145041063878)
XLA Ops:
  0.0 100.8 %shard_map.118 = bf16[4,8,64,512]{3,2,1,0:T(8,128)(2,1)} custom-call(bf16[4,8,64,512]{3,2,1,0:T(8,128)(2,1)} %bitcast.5, s32[4,8,64,512]{3,2,1,0:T(8,128)} %bitcast.4, s32[64]{0:T(128)} %first_seen_ref.1, bf16[32,512]{1,0:T(8,128)(2,1)} %pos_ref.1, bf16[2,512,512]{2,1,0:T(8,128)(2,1)} %w_struct_ref.1, bf16[2,512,512]{2,1,0:T(8,128)(2,1)} %w_query_ref.1, ...), custom_call_target="tpu_custom_call" | custom-call | tf_op jit(solution)/shard_map/pallas_call | solution.py:339
  100.8 3.0 %copy.14 = bf16[4,512,512]{2,1,0:T(8,128)(2,1)} copy(bf16[4,512,512]{2,1,0:T(8,128)(2,1)} %bitcast.3) | data formatting | bytes 4194304

commit v4 on v3

--- a/solution.py
+++ b/solution.py
@@ -32,6 +32,23 @@
 def gelu(x):
     half = 0.5 * x
     return half + half * jnp.tanh(x * (0.7978845608028654 + 0.035677408136300125 * (x * x)))
+
+
+def peers_of(me, n):
+    bits = n.bit_length() - 1
+    if 2**bits != n or bits < 3:
+        return [lax.rem(me + k, n) for k in range(1, n)]
+    digits = [(me // 2**i) % 2 for i in range(bits)]
+    core = digits[0]
+    order = sorted(range(1, n), key=lambda m: (m < 2, bin(m // 2).count("1"), m))
+    peers = []
+    for m in order:
+        flips = [(m // 2**i) % 2 for i in range(bits)]
+        low, high = flips[1], flips[2]
+        flips[1] = low * (1 - core) + high * core
+        flips[2] = high * (1 - core) + low * core
+        peers.append(sum(((d + f) % 2) * 2**i for i, (d, f) in enumerate(zip(digits, flips))))
+    return peers
 
 
 def kernel(
@@ -65,6 +82,7 @@
     bias,
     inner,
     in_sems,
+    first_sems,
     link_sems,
     go_send,
     go_recv,
@@ -89,7 +107,6 @@
         )
 
     moves = [
-        (features_ref, hidden.at[0]),
         (w_struct_ref, ws),
         (w_query_ref, wqkv.at[:, :, pl.ds(0, width)]),
         (w_key_ref, wqkv.at[:, :, pl.ds(width, width)]),
@@ -101,12 +118,24 @@
     loads = [
         pltpu.make_async_copy(src, dst, in_sems.at[i]) for i, (src, dst) in enumerate(moves)
     ]
-    loads[0].start()
-    load_links(0).start()
-    loads[1].start()
+    first = pl.ds(0, CHUNK)
+    first_loads = [
+        (
+            pltpu.make_async_copy(features_ref.at[s], hidden.at[0, s], first_sems.at[s, 0]),
+            pltpu.make_async_copy(
+                adjacency_ref.at[s, :, first], adjacent.at[s, :, first], first_sems.at[s, 1]
+            ),
+        )
+        for s in range(local)
+    ]
+    for s, pair in enumerate(first_loads):
+        for load in pair:
+            load.start()
+        if s == 0:
+            loads[0].start()
     for c in range(1, chunks):
         load_links(c).start()
-    for load in loads[2:]:
+    for load in loads[1:]:
         load.start()
 
     barrier = pltpu.get_barrier_semaphore()
@@ -147,7 +176,25 @@
             finished.at[b, c, pl.ds(peer * local, local)],
             target.at[:, me, pl.ds(c * CHUNK, CHUNK)],
             back_send.at[b],
-            back_recv.at[b],
+            back_recv.at[b, local],
+            peer,
+        )
+
+    def go_one(b, s, peer):
+        return send(
+            conv.at[b, 0, peer, pl.ds(s, 1)],
+            arrived.at[b, 0, pl.ds(me * local + s, 1)],
+            go_send.at[b],
+            go_recv.at[b, 0],
+            peer,
+        )
+
+    def back_one(b, s, peer, target):
+        return send(
+            finished.at[b, chunks - 1, pl.ds(peer * local + s, 1)],
+            target.at[pl.ds(s, 1), me, pl.ds((chunks - 1) * CHUNK, CHUNK)],
+            back_send.at[b],
+            back_recv.at[b, s],
             peer,
         )
 
@@ -155,20 +202,25 @@
         view = arrived.at[b, c, pl.ds(0, (n - 1) * local)]
         send(view, view, go_send.at[b], go_recv.at[b, c], me).wait_recv()
 
-    def await_back(b, target):
-        view = target.at[:, others]
-        send(view, view, back_send.at[b], back_recv.at[b], me).wait_recv()
+    def await_early(b, target):
+        if chunks > 1:
+            view = target.at[:, others, pl.ds(0, (chunks - 1) * CHUNK)]
+            send(view, view, back_send.at[b], back_recv.at[b, local], me).wait_recv()
+
+    def await_late(b, s, target):
+        view = target.at[pl.ds(s, 1), others, pl.ds((chunks - 1) * CHUNK, CHUNK)]
+        send(view, view, back_send.at[b], back_recv.at[b, s], me).wait_recv()
 
     def await_sent(b):
         view = conv.at[b, :, others]
         send(view, view, go_send.at[b], go_recv.at[b, 0], me).wait_send()
         view = finished.at[b, :, pl.ds(0, (n - 1) * local)]
-        send(view, view, back_send.at[b], back_recv.at[b], me).wait_send()
-
-    def convolve(b, c):
+        send(view, view, back_send.at[b], back_recv.at[b, 0], me).wait_send()
+
+    def convolve(b, c, snapshots):
         mine = pl.ds(c * CHUNK, CHUNK)
         blended, own_rows = [], []
-        for s in range(local):
+        for s in snapshots:
             links = adjacent[s, :, mine, :].reshape(n * CHUNK, nodes).astype(F32)
             degree = 1.0 + jnp.sum(links, axis=-1, keepdims=True)
             own = hidden[b, s, :, mine, :].reshape(n * CHUNK, width).astype(F32)
@@ -178,9 +230,9 @@
         projected = matmul(jnp.concatenate(blended, axis=0), ws[b])
         projected = jnp.where(projected > 0, projected, jnp.exp(jnp.minimum(projected, 0.0)) - 1.0)
         result = (projected + jnp.concatenate(own_rows, axis=0)).astype(BF16)
-        result = result.reshape(local, n, CHUNK, width)
-        for s in range(local):
-            conv[b, c, :, s] = result[s]
+        result = result.reshape(len(snapshots), n, CHUNK, width)
+        for i, s in enumerate(snapshots):
+            conv[b, c, :, s] = result[i]
 
     def mask_of(c, g):
         lane = lax.broadcasted_iota(jnp.int32, (1, rows), 1)
@@ -267,31 +319,53 @@
         finished[b, c] = jnp.concatenate(results, axis=1).astype(BF16)
 
     last = blocks - 1
-    peers = [lax.rem(me + k, n) for k in range(1, n)]
-    loads[0].wait()
-    loads[1].wait()
+    peers = peers_of(me, n)
+    own = pl.ds(me * local, local)
 
     @pl.loop(0, blocks)
     def _(b):
-        @pl.loop(0, chunks)
+        @pl.when(b > 0)
+        def _():
+            await_early(b - 1, hidden.at[b])
+
+        for s in range(local):
+
+            @pl.when(b == 0)
+            def _():
+                for load in first_loads[s]:
+                    load.wait()
+                if s == 0:
+                    loads[0].wait()
+
+            @pl.when(b > 0)
+            def _():
+                await_late(b - 1, s, hidden.at[b])
+
+            convolve(b, 0, [s])
+            if s == 0:
+
+                @pl.when(b == 0)
+                def _():
+                    pl.semaphore_wait(barrier, n - 1)
+
+            for peer in peers:
+                go_one(b, s, peer).start()
+        arrived[b, 0, own] = conv[b, 0, me]
+
+        @pl.loop(1, chunks)
         def _(c):
             @pl.when(b == 0)
             def _():
                 load_links(c).wait()
 
-            convolve(b, c)
-
-            @pl.when((b == 0) & (c == 0))
-            def _():
-                pl.semaphore_wait(barrier, n - 1)
-
+            convolve(b, c, range(local))
             for peer in peers:
                 go(b, c, peer).start()
-            arrived[b, c, pl.ds(me * local, local)] = conv[b, c, me]
+            arrived[b, c, own] = conv[b, c, me]
 
         @pl.when(b == 0)
         def _():
-            for load in loads[2:]:
+            for load in loads[1:]:
                 load.wait()
 
         @pl.loop(0, chunks)
@@ -299,29 +373,36 @@
             await_chunk(b, c)
             temporal(b, c)
             part = pl.ds(c * CHUNK, CHUNK)
-            own = pl.ds(me * local, local)
+
+            def send_back(target):
+                @pl.when(c < chunks - 1)
+                def _():
+                    for peer in peers:
+                        back(b, c, peer, target).start()
+
+                @pl.when(c == chunks - 1)
+                def _():
+                    for s in range(local):
+                        for peer in peers:
+                            back_one(b, s, peer, target).start()
 
             @pl.when(b < last)
             def _():
-                for peer in peers:
-                    back(b, c, peer, hidden.at[b + 1]).start()
+                send_back(hidden.at[b + 1])
                 hidden[b + 1, :, me, part, :] = finished[b, c, own]
 
             @pl.when(b == last)
             def _():
-                for peer in peers:
-                    back(b, c, peer, out_ref).start()
+                send_back(out_ref)
                 pltpu.make_async_copy(
                     finished.at[b, c, own], out_ref.at[:, me, part], out_sem
                 ).start()
 
-        @pl.when(b < last)
-        def _():
-            await_back(b, hidden.at[b + 1])
-
     for b in range(blocks):
         await_sent(b)
-    await_back(last, out_ref)
+    await_early(last, out_ref)
+    for s in range(local):
+        await_late(last, s, out_ref)
     pltpu.make_async_copy(
         finished.at[last, :, pl.ds(0, local)], finished.at[last, :, pl.ds(0, local)], out_sem
     ).wait()
@@ -364,12 +445,13 @@
             pltpu.VMEM((chunk_rows, width), BF16),
             pltpu.VMEM((CHUNK // GROUP, steps * GROUP, steps * GROUP), F32),
             pltpu.VMEM((chunk_rows, hidden_units), BF16),
-            pltpu.SemaphoreType.DMA((8,)),
+            pltpu.SemaphoreType.DMA((7,)),
+            pltpu.SemaphoreType.DMA((local, 2)),
             pltpu.SemaphoreType.DMA((chunks,)),
             pltpu.SemaphoreType.DMA((blocks,)),
             pltpu.SemaphoreType.DMA((blocks, chunks)),
             pltpu.SemaphoreType.DMA((blocks,)),
-            pltpu.SemaphoreType.DMA((blocks,)),
+            pltpu.SemaphoreType.DMA((blocks, local + 1)),
             pltpu.SemaphoreType.DMA,
         ],
         compiler_params=pltpu.CompilerParams(

time: 105 us -> 102 us (0.971)
  Pallas kernels: 101 us -> 98.2 us
    pallas_call x1, Pallas kernels: 101 us -> 98.2 us  [on_device(): pl.pallas_call(functools.partial(kernel, n), out_shape=jax.ShapeDtypeStru...]
where the time goes in v4:
time: 102 us; the launch traced here: 101 us
  Pallas kernels  98.2 us (96%)
  local copies, waits for them, and re-layouts  3.05 us (3%)
    pallas_call x1, Pallas kernels, on_device(): pl.pallas_call(functools.partial(kernel, n), out_shape=jax.ShapeDtypeStru...  98.2 us
    unnamed x1, local copies, waits for them, and re-layouts  3.05 us

profile of v4, /device:TPU:0, one launch (start us, length us, event | category | flops | bytes accessed | tf_op | source)
XLA Modules:
  0.0 101.3 jit_solution(7484996634349411260)
XLA Ops:
  0.0 98.2 %shard_map.118 = bf16[4,8,64,512]{3,2,1,0:T(8,128)(2,1)} custom-call(bf16[4,8,64,512]{3,2,1,0:T(8,128)(2,1)} %bitcast.5, s32[4,8,64,512]{3,2,1,0:T(8,128)} %bitcast.4, s32[64]{0:T(128)} %first_seen_ref.1, bf16[32,512]{1,0:T(8,128)(2,1)} %pos_ref.1, bf16[2,512,512]{2,1,0:T(8,128)(2,1)} %w_struct_ref.1, bf16[2,512,512]{2,1,0:T(8,128)(2,1)} %w_query_ref.1, ...), custom_call_target="tpu_custom_call" | custom-call | tf_op jit(solution)/shard_map/pallas_call | solution.py:420
  98.2 3.0 %copy.14 = bf16[4,512,512]{2,1,0:T(8,128)(2,1)} copy(bf16[4,512,512]{2,1,0:T(8,128)(2,1)} %bitcast.3) | data formatting | bytes 4194304

commit v5 on v4

--- a/solution.py
+++ b/solution.py
@@ -406,6 +406,16 @@
     pltpu.make_async_copy(
         finished.at[last, :, pl.ds(0, local)], finished.at[last, :, pl.ds(0, local)], out_sem
     ).wait()
+
+
+def hand_over(rows_ref, out_ref, sem):
+    local, n = rows_ref.shape[:2]
+    cuts = (0, n // 2, n)
+    for s in range(local):
+        for start, end in zip(cuts, cuts[1:]):
+            part = pl.ds(start, end - start)
+            pltpu.make_async_copy(rows_ref.at[s, part], out_ref.at[s, part], sem).start()
+    pltpu.make_async_copy(rows_ref, out_ref, sem).wait()
 
 
 def on_device(n, features, adjacency, first_seen, pos_embed, *weights):
@@ -464,6 +474,14 @@
         pos_embed,
         *weights,
     )
+    result = pl.pallas_call(
+        hand_over,
+        out_shape=jax.ShapeDtypeStruct(result.shape, BF16),
+        in_specs=[anywhere],
+        out_specs=anywhere,
+        scratch_shapes=[pltpu.SemaphoreType.DMA],
+        compiler_params=pltpu.CompilerParams(vmem_limit_bytes=56 * 2**20),
+    )(result)
     return result.reshape(local, nodes, width)
 
 

time: 102 us -> 163 us (1.60)
  Pallas kernels: 98.2 us -> 163 us
  local copies, waits for them, and re-layouts: 3.05 us -> 0 us
    pallas_call x0 -> x1, Pallas kernels: none -> 64.6 us  [on_device(): pl.pallas_call(hand_over, out_shape=jax.ShapeDtypeStruct(result.shape, BF...]
    unnamed x1 -> x0, local copies, waits for them, and re-layouts: 3.05 us -> none
where the time goes in v5:
time: 163 us
  Pallas kernels  163 us (100%)
    pallas_call x1, Pallas kernels, on_device(): pl.pallas_call(functools.partial(kernel, n), out_shape=jax.ShapeDtypeStru...  98.2 us
    pallas_call x1, Pallas kernels, on_device(): pl.pallas_call(hand_over, out_shape=jax.ShapeDtypeStruct(result.shape, BF...  64.6 us

profile of v5, /device:TPU:0, one launch (start us, length us, event | category | flops | bytes accessed | tf_op | source)
XLA Modules:
  0.0 162.9 jit_solution(15851977821343677343)
XLA Ops:
  0.0 98.2 %shard_map.118.rows_ref = bf16[4,8,64,512]{3,2,1,0:T(8,128)(2,1)} custom-call(bf16[4,8,64,512]{3,2,1,0:T(8,128)(2,1)} %bitcast.4, s32[4,8,64,512]{3,2,1,0:T(8,128)} %bitcast.3, s32[64]{0:T(128)} %first_seen_ref.1, bf16[32,512]{1,0:T(8,128)(2,1)} %pos_ref.1, bf16[2,512,512]{2,1,0:T(8,128)(2,1)} %w_struct_ref.1, bf16[2,512,512]{2,1,0:T(8,128)(2,1)} %w_query_ref.1, ...), custom_call_target="tpu_custom_call" | custom-call | tf_op jit(solution)/shard_map/pallas_call | solution.py:430
  98.2 64.6 %shard_map.119 = bf16[4,8,64,512]{3,2,1,0:T(8,128)(2,1)} custom-call(bf16[4,8,64,512]{3,2,1,0:T(8,128)(2,1)} %shard_map.118.rows_ref), custom_call_target="tpu_custom_call" | custom-call | tf_op jit(solution)/shard_map/pallas_call | solution.py:477
